TPU v7x, 32 devices: a whole 2x2x4 slice. The times are simulated.
32 devices in a mesh: dp: 4 (over z), fsdp: 8 (over y, x, core).
Axes of the slice: x: 2, y: 2, z: 4, core: 2. Of those that a mesh axis runs over, the one named last changes fastest.
Arguments:
- item_hidden: bfloat16 [2048, 2048], P(('dp', 'fsdp')), may hold values from -400 to 400
- item_gain: float32 [2048], replicated, may hold values from 0.25 to 1.75
- history: int32 [4096], P(('dp', 'fsdp')), may hold values from 0 to 255, as said below
- owner_map: int32 [8, 256], P('fsdp'), may hold values from 0 to 255, as said below
- user_gain: float32 [2048], replicated, may hold values from 0.25 to 1.75
- value_weight: bfloat16 [2048, 2048], P('fsdp'), may hold values from -0.125 to 0.125
- value_grad: bfloat16 [4096, 2048], P(('dp', 'fsdp')), may hold values from -6 to 6
Outputs:
- values: bfloat16 [4096, 2048], P(('dp', 'fsdp'))
- item_grad: float32 [2048, 2048], P(('dp', 'fsdp'))
Inputs may be any that keep to these rules, and one draw needn't show every extreme that they name: `history`: storage row s of catalog c is row s % 64 of the items on dp index s // 64 and fsdp index c. In each aligned block of 128 positions, the positions name at most 8 distinct items stored on any one dp index, and exactly 8 for some dp index. `owner_map`: each row is a permutation.
All inputs are finite; a program needn't handle non-finite values.
Results may differ from a plain program's by a relative error of at most 0.0057.
Values may be sent and summed in bfloat16 or wider, within the bound.
A program may use at most 64 MiB of HBM per device.

v0:
```python
import functools
import jax
import jax.numpy as jnp
from jax import lax
from jax.experimental import pallas as pl
from jax.experimental.pallas import tpu as pltpu
from jax.sharding import PartitionSpec as P

CAP = 8
MESH = pl.DeviceIdType.MESH
f32 = jnp.float32
bf16 = jnp.bfloat16


eps = 1e-06


def norm_rows(values, gain):
    scale = lax.rsqrt(jnp.mean(values * values, axis=1, keepdims=True) + eps)
    return (values * scale * gain, scale)


def norm_back(values, gain, scale, upstream):
    unit = values * scale
    scaled = upstream * gain
    return scale * (scaled - unit * jnp.mean(scaled * unit, axis=1, keepdims=True))


def locate(owner_row, items):
    matches = items[:, None] == lax.broadcasted_iota(
        jnp.int32, (items.shape[0], owner_row.shape[0]), 1
    )
    return jnp.sum(jnp.where(matches, owner_row[None, :], 0), axis=1)


def local_moving_weight(item_hidden, item_gain, history, owner_map, user_gain, value_weight, value_grad):
    groups = lax.axis_size("dp")
    here = lax.axis_index("dp")
    item_rows = item_hidden.shape[0]
    hist_rows = history.shape[0]
    width = item_hidden.shape[1]
    owner_row = owner_map[0]
    pool = owner_row.shape[0]
    hidden = item_hidden.astype(jnp.float32)
    item_emb, item_scale = norm_rows(hidden, item_gain)
    item_emb = item_emb.astype(jnp.bfloat16)
    all_history = lax.all_gather(history, "dp", axis=0, tiled=True)
    stored_all = locate(owner_row, all_history).reshape(groups, hist_rows)
    local_rows = lax.broadcasted_iota(jnp.int32, (groups, hist_rows, item_rows), 2)
    wanted = jnp.any(stored_all[:, :, None] == here * item_rows + local_rows, axis=1)
    slot = jnp.cumsum(wanted.astype(jnp.int32), axis=1) - 1
    slot_ids = lax.broadcasted_iota(jnp.int32, (groups, CAP, item_rows), 1)
    select = (wanted[:, None, :] & (slot[:, None, :] == slot_ids)).astype(jnp.bfloat16)
    outgoing = jnp.einsum(
        "dcr,rk->dck", select, item_emb, preferred_element_type=jnp.float32
    ).astype(jnp.bfloat16)
    incoming = lax.all_to_all(outgoing, "dp", split_axis=0, concat_axis=0, tiled=True)
    stored = locate(owner_row, history)
    pick = stored[:, None] == lax.broadcasted_iota(jnp.int32, (hist_rows, pool), 1)
    own_wanted = jnp.any(pick, axis=0).reshape(groups, item_rows)
    own_slot = (jnp.cumsum(own_wanted.astype(jnp.int32), axis=1) - 1).reshape(pool)
    slot_pos = jnp.sum(jnp.where(pick, own_slot[None, :], 0), axis=1)
    buffer_row = stored // item_rows * CAP + slot_pos
    x = jnp.take(incoming.reshape(groups * CAP, width), buffer_row, axis=0).astype(jnp.float32)
    normed, scale = norm_rows(x, user_gain)
    normed = normed.astype(jnp.bfloat16)
    whole = lax.all_gather(value_weight, "fsdp", axis=0, tiled=True)
    values = jnp.dot(normed, whole, preferred_element_type=jnp.float32)
    upstream = lax.dot_general(
        value_grad, whole, (((1,), (1,)), ((), ())), preferred_element_type=jnp.float32
    )
    values = values.astype(jnp.bfloat16)
    dx = norm_back(x, user_gain, scale, upstream)
    one_hot = (
        buffer_row[:, None] == lax.broadcasted_iota(jnp.int32, (hist_rows, groups * CAP), 1)
    ).astype(jnp.float32)
    summed = lax.dot_general(
        one_hot,
        dx,
        (((0,), (0,)), ((), ())),
        precision=lax.Precision.HIGHEST,
        preferred_element_type=jnp.float32,
    )
    returned = lax.all_to_all(
        summed.astype(jnp.bfloat16).reshape(groups, CAP, width),
        "dp",
        split_axis=0,
        concat_axis=0,
        tiled=True,
    )
    emb_grad = jnp.einsum("dcr,dck->rk", select, returned, preferred_element_type=jnp.float32)
    item_grad = norm_back(hidden, item_gain, item_scale, emb_grad)
    return (values, item_grad)


CHUNKS = 4


def iota(shape, dim):
    return lax.broadcasted_iota(jnp.int32, shape, dim)


def dot(a, b, ca=1, cb=0):
    return lax.dot_general(a, b, (((ca,), (cb,)), ((), ())), preferred_element_type=f32)


def fold(rows):
    half = rows.shape[1] // 2
    return jnp.concatenate([rows[:, :half], rows[:, half:]], axis=0)


def unfold(rows):
    return jnp.concatenate([rows[:CAP], rows[CAP:]], axis=1)


def stored_rows(hist, parts, item_rows):
    pool = parts.shape[1]
    named = (iota((pool, hist.shape[1]), 0) == hist).astype(f32).astype(bf16)
    found = dot(parts, named)
    return found[0:1] * item_rows + found[1:2]


def slots(wants, item_rows):
    lane = iota((item_rows, 128), 1)
    wanted = jnp.zeros((item_rows, 128), f32)
    for group, want in enumerate(wants):
        wanted = jnp.where(lane // CAP == group, want, wanted)
    before = (iota((item_rows, item_rows), 1) < iota((item_rows, item_rows), 0)).astype(f32)
    slot = dot(before.astype(bf16), wanted.astype(bf16))
    return jnp.where(slot == (lane % CAP).astype(f32), wanted, 0.0)


def kernel(
    groups, chips,
    item_gain_hbm, history_hbm, owner_hbm, user_gain_hbm, item_hidden, weight, value_grad,
    back_in, total_out, place_out, select_out,
    item_gain, history, owner, user_gain,
    hidden_buf, grad_buf, w_buf, hist_buf, emb_out, emb_in, sum_buf, x_out, x_in,
    part_own, part_out, part_in, up_out, up_in, back_out, total_buf, place_buf, select_buf,
    local_sem, out_sem, w_sem, hello, hist_send, hist_recv, emb_send, emb_recv, sum_send, sum_recv,
    x_send, x_recv, part_send, part_recv, up_send, up_recv, back_send, back_recv,
):
    here = lax.axis_index("dp")
    fsdp = lax.axis_index("fsdp")
    chip = fsdp // 2
    core = fsdp % 2
    item_rows, width = item_hidden.shape
    hist_rows = history.shape[1]
    rows = groups * CAP
    piece = width // chips
    cols = value_grad.shape[1] // CHUNKS
    peers = [lax.rem(here + k, groups) for k in range(1, groups)]
    mates = [lax.rem(chip + k, chips) for k in range(1, chips)]

    def dp_id(peer):
        return (peer, fsdp)

    def chip_id(mate):
        return (here, mate * 2 + core)

    sibling = (here, chip * 2 + 1 - core)

    barrier = pltpu.get_barrier_semaphore()
    group = [dp_id(p) for p in peers] + [chip_id(m) for m in mates]
    for target in group:
        pl.semaphore_signal(barrier, inc=1, device_id=target, device_id_type=MESH)

    loads = [
        pltpu.make_async_copy(src, dst, local_sem.at[k])
        for k, (src, dst) in enumerate([
            (history_hbm, history), (owner_hbm, owner), (value_grad, grad_buf),
            (item_hidden, hidden_buf), (item_gain_hbm, item_gain),
            (user_gain_hbm, user_gain), (weight, w_buf.at[core]),
        ])
    ]
    for load in loads:
        load.start()

    @pl.when(core == 0)
    def _():
        pl.semaphore_wait(barrier, len(group))
        pl.semaphore_signal(barrier, inc=1, device_id=sibling, device_id_type=MESH)

    @pl.when(core == 1)
    def _():
        pl.semaphore_wait(barrier, len(group) + 1)
        pl.semaphore_signal(hello, inc=1, device_id=sibling, device_id_type=MESH)

    w_copy = pltpu.make_async_remote_copy(
        src_ref=weight, dst_ref=w_buf.at[core], send_sem=w_sem.at[0], recv_sem=w_sem.at[1],
        device_id=sibling, device_id_type=MESH,
    )

    @pl.when(core == 1)
    def _():
        w_copy.start()

    def remote(src, dst, send, recv, target):
        return pltpu.make_async_remote_copy(
            src_ref=src, dst_ref=dst, send_sem=send, recv_sem=recv,
            device_id=target, device_id_type=MESH,
        )

    sends = []

    def send_dp(out_of, into, send, recv):
        for k, peer in enumerate(peers):
            copy = remote(out_of(peer), into.at[here], send.at[k], recv.at[here], dp_id(peer))
            copy.start()
            sends.append(copy)

    def wait_dp(into, send, recv):
        for k, peer in enumerate(peers):
            remote(into.at[peer], into.at[peer], send.at[k], recv.at[peer], dp_id(peer)).wait_recv()

    def send_chip(out_of, into, send, recv):
        for k, mate in enumerate(mates):
            copy = remote(out_of(mate), into.at[chip], send.at[k], recv.at[chip], chip_id(mate))
            copy.start()
            sends.append(copy)

    def wait_chip(into, send, recv):
        for k, mate in enumerate(mates):
            remote(into.at[mate], into.at[mate], send.at[k], recv.at[mate], chip_id(mate)).wait_recv()

    loads[0].wait()
    send_dp(lambda peer: history, hist_buf, hist_send, hist_recv)
    hist_buf[here] = history[...]

    loads[1].wait()
    owner_row = owner[...]
    pool = owner_row.shape[1]
    div = (owner_row // item_rows).astype(f32)
    mod = (owner_row % item_rows).astype(f32)
    parts = jnp.where(iota((8, pool), 0) == 0, div, mod).astype(bf16)

    own = stored_rows(history[...], parts, item_rows)
    match = (iota((pool, hist_rows), 0).astype(f32) == own).astype(f32)
    wants = [
        jnp.max(match[e * item_rows : (e + 1) * item_rows], axis=1, keepdims=True)
        for e in range(groups)
    ]
    one_hot = slots(wants, item_rows)
    lane = iota((item_rows, 128), 1)
    stacked = jnp.concatenate(
        [jnp.where(lane // CAP == e, one_hot, 0.0) for e in range(groups)], axis=0
    )
    place = dot(stacked.astype(bf16), match.astype(bf16), 0, 0)[:rows]
    place = place.astype(bf16)
    place_buf[...] = place
    outs = [pltpu.make_async_copy(place_buf, place_out, out_sem.at[0])]
    outs[0].start()

    loads[2].wait()
    for c in range(CHUNKS):
        sum_buf[c, chip] = dot(place, grad_buf[:, c * cols : (c + 1) * cols]).astype(bf16)
        send_chip(
            lambda mate: sum_buf.at[c, chip], sum_buf.at[c], sum_send.at[c], sum_recv.at[c]
        )

    loads[3].wait()
    loads[4].wait()
    hidden = hidden_buf[...].astype(f32)
    item_scale = lax.rsqrt(jnp.mean(hidden * hidden, axis=1, keepdims=True) + 1e-6)
    item_emb = (hidden * item_scale * item_gain[...]).astype(bf16)

    wait_dp(hist_buf, hist_send, hist_recv)
    base = (here * item_rows).astype(f32)
    local_rows = iota((item_rows, hist_rows), 0).astype(f32) + base
    wants = []
    for t in range(groups):
        stored = stored_rows(hist_buf[t], parts, item_rows)
        wants.append(jnp.max((local_rows == stored).astype(f32), axis=1, keepdims=True))
    select = slots(wants, item_rows)[:, :rows].astype(bf16)
    select_buf[...] = select
    outs.append(pltpu.make_async_copy(select_buf, select_out, out_sem.at[1]))
    outs[1].start()
    outgoing = dot(select, item_emb, 0, 0)
    for t in range(groups):
        emb_out[t] = fold(outgoing[t * CAP : (t + 1) * CAP]).astype(bf16)
    send_dp(lambda peer: emb_out.at[peer], emb_in, emb_send, emb_recv)
    emb_in[here] = emb_out[here]

    @pl.when(core == 0)
    def _():
        pl.semaphore_wait(hello, 1)
        w_copy.start()

    loads[5].wait()
    wait_dp(emb_in, emb_send, emb_recv)

    x = jnp.concatenate([unfold(emb_in[e].astype(f32)) for e in range(groups)], axis=0)
    scale = lax.rsqrt(jnp.mean(x * x, axis=1, keepdims=True) + 1e-6)
    normed = (x * scale * user_gain[...]).astype(bf16)
    for p in range(chips):
        x_out[p] = normed[:, p * piece : (p + 1) * piece]
    send_chip(lambda mate: x_out.at[mate], x_in, x_send, x_recv)
    x_in[chip] = x_out[chip]

    loads[6].wait()
    w_copy.wait()
    w_all = w_buf[...].reshape(piece, -1)

    up = jnp.zeros((chips * rows, piece), f32)
    for c in range(CHUNKS):
        wait_chip(sum_buf.at[c], sum_send.at[c], sum_recv.at[c])
        sums = sum_buf[c].reshape(chips * rows, cols)
        up = up + dot(sums, w_all[:, c * cols : (c + 1) * cols], 1, 1)
    up_out[...] = up.reshape(chips, rows, piece)
    send_chip(lambda mate: up_out.at[mate], up_in, up_send, up_recv)
    up_in[chip] = up_out[chip]

    wait_chip(x_in, x_send, x_recv)
    x_all = x_in[...].reshape(chips * rows, piece)
    for c in range(CHUNKS):
        part = dot(x_all, w_all[:, c * cols : (c + 1) * cols]).reshape(chips, rows, cols)
        part_own[c] = part
        part_out[c] = part.astype(bf16)
        send_chip(
            lambda mate: part_out.at[c, mate], part_in.at[c], part_send.at[c], part_recv.at[c]
        )

    wait_chip(up_in, up_send, up_recv)
    upstream = jnp.concatenate([up_in[p] for p in range(chips)], axis=1)
    unit = x * scale
    scaled = upstream * user_gain[...]
    block_sum = scale * (scaled - unit * jnp.mean(scaled * unit, axis=1, keepdims=True))
    for t in range(groups):
        back_out[t] = fold(block_sum[t * CAP : (t + 1) * CAP]).astype(bf16)
    send_dp(lambda peer: back_out.at[peer], back_in, back_send, back_recv)
    outs.append(pltpu.make_async_copy(back_out.at[here], back_in.at[here], out_sem.at[2]))
    outs[2].start()

    for c in range(CHUNKS):
        wait_chip(part_in.at[c], part_send.at[c], part_recv.at[c])
        total = part_own[c, chip]
        for mate in mates:
            total = total + part_in[c, mate].astype(f32)
        total_buf[c] = total.astype(bf16)
        out = pltpu.make_async_copy(total_buf.at[c], total_out.at[c], out_sem.at[3 + c])
        out.start()
        outs.append(out)

    wait_dp(back_in, back_send, back_recv)
    for out in outs:
        out.wait()
    for copy in sends:
        copy.wait_send()


def finish(
    groups, back_hbm, total_hbm, place_hbm, select_hbm, hidden_hbm, gain_hbm,
    values_out, item_grad_out,
    back, total, place, select, hidden_buf, gain, values, item_grad, load_sem, out_sem,
):
    loads = [
        pltpu.make_async_copy(src, dst, load_sem.at[k])
        for k, (src, dst) in enumerate([
            (hidden_hbm, hidden_buf), (gain_hbm, gain), (select_hbm, select), (back_hbm, back),
            (place_hbm, place), (total_hbm, total),
        ])
    ]
    for load in loads:
        load.start()
    loads[0].wait()
    loads[1].wait()
    hidden = hidden_buf[...].astype(f32)
    scale = lax.rsqrt(jnp.mean(hidden * hidden, axis=1, keepdims=True) + 1e-6)
    loads[2].wait()
    loads[3].wait()
    returned = jnp.concatenate([unfold(back[t].astype(f32)) for t in range(groups)], axis=0)
    emb_grad = dot(select[...], returned.astype(bf16))
    unit = hidden * scale
    scaled = emb_grad * gain[...]
    item_grad[...] = scale * (scaled - unit * jnp.mean(scaled * unit, axis=1, keepdims=True))
    grad_copy = pltpu.make_async_copy(item_grad, item_grad_out, out_sem.at[0])
    grad_copy.start()
    loads[4].wait()
    loads[5].wait()
    named = place[...]
    cols = total.shape[2]
    for c in range(CHUNKS):
        values[:, c * cols : (c + 1) * cols] = dot(named, total[c], 0, 0).astype(bf16)
    values_copy = pltpu.make_async_copy(values, values_out, out_sem.at[1])
    values_copy.start()
    grad_copy.wait()
    values_copy.wait()


def local_moving_rows(
    item_hidden, item_gain, history, owner_map, user_gain, value_weight, value_grad
):
    groups = lax.axis_size("dp")
    chips = lax.axis_size("fsdp") // 2
    item_rows, width = item_hidden.shape
    hist_rows, out_width = value_grad.shape
    rows = groups * CAP
    depth = value_weight.shape[0]
    piece = 2 * depth
    cols = out_width // CHUNKS
    hbm = pl.BlockSpec(memory_space=pl.ANY)

    def dma(*counts):
        return pltpu.SemaphoreType.DMA(counts)

    folded = (groups, 2 * CAP, width // 2)
    back, total, place, select = pl.pallas_call(
        functools.partial(kernel, groups, chips),
        out_shape=(
            jax.ShapeDtypeStruct(folded, bf16),
            jax.ShapeDtypeStruct((CHUNKS, rows, cols), bf16),
            jax.ShapeDtypeStruct((rows, hist_rows), bf16),
            jax.ShapeDtypeStruct((item_rows, rows), bf16),
        ),
        in_specs=[hbm] * 7,
        out_specs=(hbm,) * 4,
        scratch_shapes=[
            pltpu.VMEM((1, width), f32),
            pltpu.VMEM((1, hist_rows), jnp.int32),
            pltpu.VMEM((1, owner_map.shape[1]), jnp.int32),
            pltpu.VMEM((1, width), f32),
            pltpu.VMEM((item_rows, width), bf16),
            pltpu.VMEM((hist_rows, out_width), bf16),
            pltpu.VMEM((2, depth, out_width), bf16),
            pltpu.VMEM((groups, 1, hist_rows), jnp.int32),
            pltpu.VMEM(folded, bf16),
            pltpu.VMEM(folded, bf16),
            pltpu.VMEM((CHUNKS, chips, rows, cols), bf16),
            pltpu.VMEM((chips, rows, piece), bf16),
            pltpu.VMEM((chips, rows, piece), bf16),
            pltpu.VMEM((CHUNKS, chips, rows, cols), f32),
            pltpu.VMEM((CHUNKS, chips, rows, cols), bf16),
            pltpu.VMEM((CHUNKS, chips, rows, cols), bf16),
            pltpu.VMEM((chips, rows, piece), f32),
            pltpu.VMEM((chips, rows, piece), f32),
            pltpu.VMEM(folded, bf16),
            pltpu.VMEM((CHUNKS, rows, cols), bf16),
            pltpu.VMEM((rows, hist_rows), bf16),
            pltpu.VMEM((item_rows, rows), bf16),
            dma(7), dma(3 + CHUNKS), dma(2), pltpu.SemaphoreType.REGULAR,
            dma(groups), dma(groups), dma(groups), dma(groups),
            dma(CHUNKS, chips), dma(CHUNKS, chips), dma(chips), dma(chips),
            dma(CHUNKS, chips), dma(CHUNKS, chips), dma(chips), dma(chips),
            dma(groups), dma(groups),
        ],
        compiler_params=pltpu.CompilerParams(
            collective_id=0, has_side_effects=True, vmem_limit_bytes=60 * 2**20
        ),
    )(
        item_gain[None, :], history[None, :], owner_map, user_gain[None, :],
        item_hidden, value_weight, value_grad,
    )
    return pl.pallas_call(
        functools.partial(finish, groups),
        out_shape=(
            jax.ShapeDtypeStruct((hist_rows, out_width), bf16),
            jax.ShapeDtypeStruct((item_rows, width), f32),
        ),
        in_specs=[hbm] * 6,
        out_specs=(hbm,) * 2,
        scratch_shapes=[
            pltpu.VMEM(folded, bf16),
            pltpu.VMEM((CHUNKS, rows, cols), bf16),
            pltpu.VMEM((rows, hist_rows), bf16),
            pltpu.VMEM((item_rows, rows), bf16),
            pltpu.VMEM((item_rows, width), bf16),
            pltpu.VMEM((1, width), f32),
            pltpu.VMEM((hist_rows, out_width), bf16),
            pltpu.VMEM((item_rows, width), f32),
            dma(6), dma(2),
        ],
        compiler_params=pltpu.CompilerParams(vmem_limit_bytes=60 * 2**20),
    )(back, total, place, select, item_hidden, item_gain[None, :])


def local(item_hidden, item_gain, history, owner_map, user_gain, value_weight, value_grad):
    chips = lax.axis_size("fsdp") // 2
    moved = 2 * chips * lax.axis_size("dp") * CAP
    by_rows = moved <= value_grad.shape[1] and lax.axis_size("dp") * CAP <= 128
    plan = local_moving_rows if by_rows else local_moving_weight
    return plan(
        item_hidden, item_gain, history, owner_map, user_gain, value_weight, value_grad
    )


def solution(mesh):
    in_specs = (
        P(("dp", "fsdp"), None),
        P(),
        P(("dp", "fsdp")),
        P("fsdp", None),
        P(),
        P("fsdp", None),
        P(("dp", "fsdp"), None),
    )
    out_specs = (P(("dp", "fsdp"), None), P(("dp", "fsdp"), None))
    return jax.shard_map(local, mesh=mesh, in_specs=in_specs, out_specs=out_specs, check_vma=False)
```

profile of v0, /device:TPU:0, one launch (start us, length us, event | category | flops | bytes accessed | tf_op | source)
XLA Modules:
  0.0 30.6 jit_solution(9229721076327992917)
XLA Ops:
  0.6 27.3 %shard_map.86 = (bf16[4,16,1024]{2,1,0:T(8,128)(2,1)}, bf16[4,32,512]{2,1,0:T(8,128)(2,1)}, bf16[32,128]{1,0:T(8,128)(2,1)}, bf16[64,32]{1,0:T(8,128)(2,1)}) custom-call(f32[1,2048]{1,0:T(1,128)} %bitcast.3, s32[1,128]{1,0:T(1,128)} %bitcast.6, s32[1,256]{1,0:T(1,128)} %owner_hbm.1, f32[1,2048]{1,0:T(1,128)} %bitcast.5, bf16[64,2048]{1,0:T(8,128)(2,1)} %hidden_hbm.1, ...), custom_call_target="tpu_custom_call" | custom-call | tf_op jit(solution)/shard_map/pallas_call | solution.py:407
  28.0 2.6 %shard_map.87 = (bf16[128,2048]{1,0:T(8,128)(2,1)}, f32[64,2048]{1,0:T(8,128)}) custom-call(bf16[4,16,1024]{2,1,0:T(8,128)(2,1)} %get-tuple-element.6.back_hbm, bf16[4,32,512]{2,1,0:T(8,128)(2,1)} %get-tuple-element.7.total_hbm, bf16[32,128]{1,0:T(8,128)(2,1)} %get-tuple-element.8.place_hbm, bf16[64,32]{1,0:T(8,128)(2,1)} %get-tuple-element.9.select_hbm, ...), custom_call_target="tpu_custom_call" | custom-call | tf_op jit(solution)/shard_map/pallas_call | solution.py:453
where the time goes:
time: 30.8 us; the launch traced here: 30.6 us
  Pallas kernels  30 us (97%)
  between operations  0.64 us (2%)
    pallas_call x1, Pallas kernels, local_moving_rows(): pl.pallas_call(functools.partial(kernel, groups, chips), out_shape=(jax.S...  27.3 us
    pallas_call x1, Pallas kernels, local_moving_rows(): pl.pallas_call(functools.partial(finish, groups), out_shape=(jax.ShapeDty...  2.62 us

commit v1 on v0

--- a/solution.py
+++ b/solution.py
@@ -93,7 +93,7 @@
     return (values, item_grad)
 
 
-CHUNKS = 4
+CHUNKS = 2
 
 
 def iota(shape, dim):
@@ -136,7 +136,7 @@
     back_in, total_out, place_out, select_out,
     item_gain, history, owner, user_gain,
     hidden_buf, grad_buf, w_buf, hist_buf, emb_out, emb_in, sum_buf, x_out, x_in,
-    part_own, part_out, part_in, up_out, up_in, back_out, total_buf, place_buf, select_buf,
+    part_own, part_out, part_in, up_out, up_in, back_out, total_buf, place_buf, select_buf, wt_buf,
     local_sem, out_sem, w_sem, hello, hist_send, hist_recv, emb_send, emb_recv, sum_send, sum_recv,
     x_send, x_recv, part_send, part_recv, up_send, up_recv, back_send, back_recv,
 ):
@@ -223,8 +223,8 @@
         for k, mate in enumerate(mates):
             remote(into.at[mate], into.at[mate], send.at[k], recv.at[mate], chip_id(mate)).wait_recv()
 
+    send_dp(lambda peer: history_hbm, hist_buf, hist_send, hist_recv)
     loads[0].wait()
-    send_dp(lambda peer: history, hist_buf, hist_send, hist_recv)
     hist_buf[here] = history[...]
 
     loads[1].wait()
@@ -286,6 +286,8 @@
         pl.semaphore_wait(hello, 1)
         w_copy.start()
 
+    loads[6].wait()
+    wt_buf[core] = w_buf[core].T
     loads[5].wait()
     wait_dp(emb_in, emb_send, emb_recv)
 
@@ -297,16 +299,18 @@
     send_chip(lambda mate: x_out.at[mate], x_in, x_send, x_recv)
     x_in[chip] = x_out[chip]
 
-    loads[6].wait()
     w_copy.wait()
+    wt_buf[1 - core] = w_buf[1 - core].T
     w_all = w_buf[...].reshape(piece, -1)
 
-    up = jnp.zeros((chips * rows, piece), f32)
+    half = piece // 2
+    ups = [jnp.zeros((chips * rows, half), f32)] * 2
     for c in range(CHUNKS):
         wait_chip(sum_buf.at[c], sum_send.at[c], sum_recv.at[c])
         sums = sum_buf[c].reshape(chips * rows, cols)
-        up = up + dot(sums, w_all[:, c * cols : (c + 1) * cols], 1, 1)
-    up_out[...] = up.reshape(chips, rows, piece)
+        ups = [ups[h] + dot(sums, wt_buf[h, c * cols : (c + 1) * cols]) for h in range(2)]
+    for h in range(2):
+        up_out[:, :, h * half : (h + 1) * half] = ups[h].reshape(chips, rows, half)
     send_chip(lambda mate: up_out.at[mate], up_in, up_send, up_recv)
     up_in[chip] = up_out[chip]
 
@@ -437,6 +441,7 @@
             pltpu.VMEM((CHUNKS, rows, cols), bf16),
             pltpu.VMEM((rows, hist_rows), bf16),
             pltpu.VMEM((item_rows, rows), bf16),
+            pltpu.VMEM((2, out_width, depth), bf16),
             dma(7), dma(3 + CHUNKS), dma(2), pltpu.SemaphoreType.REGULAR,
             dma(groups), dma(groups), dma(groups), dma(groups),
             dma(CHUNKS, chips), dma(CHUNKS, chips), dma(chips), dma(chips),

time: 30.8 us -> 30.7 us (level)
  no operation moved by 1% of the time
where the time goes in v1:
time: 30.7 us; the launch traced here: 30.6 us
  Pallas kernels  29.9 us (97%)
  between operations  0.64 us (2%)
    pallas_call x1, Pallas kernels, local_moving_rows(): pl.pallas_call(functools.partial(kernel, groups, chips), out_shape=(jax.S...  27.3 us
    pallas_call x1, Pallas kernels, local_moving_rows(): pl.pallas_call(functools.partial(finish, groups), out_shape=(jax.ShapeDty...  2.62 us

profile of v1, /device:TPU:0, one launch (start us, length us, event | category | flops | bytes accessed | tf_op | source)
XLA Modules:
  0.0 30.6 jit_solution(816638510146924806)
XLA Ops:
  0.6 27.3 %shard_map.86 = (bf16[4,16,1024]{2,1,0:T(8,128)(2,1)}, bf16[2,32,1024]{2,1,0:T(8,128)(2,1)}, bf16[32,128]{1,0:T(8,128)(2,1)}, bf16[64,32]{1,0:T(8,128)(2,1)}) custom-call(f32[1,2048]{1,0:T(1,128)} %bitcast.3, s32[1,128]{1,0:T(1,128)} %bitcast.6, s32[1,256]{1,0:T(1,128)} %owner_hbm.1, f32[1,2048]{1,0:T(1,128)} %bitcast.5, bf16[64,2048]{1,0:T(8,128)(2,1)} %hidden_hbm.1, ...), custom_call_target="tpu_custom_call" | custom-call | tf_op jit(solution)/shard_map/pallas_call | solution.py:411
  28.0 2.6 %shard_map.87 = (bf16[128,2048]{1,0:T(8,128)(2,1)}, f32[64,2048]{1,0:T(8,128)}) custom-call(bf16[4,16,1024]{2,1,0:T(8,128)(2,1)} %get-tuple-element.6.back_hbm, bf16[2,32,1024]{2,1,0:T(8,128)(2,1)} %get-tuple-element.7.total_hbm, bf16[32,128]{1,0:T(8,128)(2,1)} %get-tuple-element.8.place_hbm, bf16[64,32]{1,0:T(8,128)(2,1)} %get-tuple-element.9.select_hbm, ...), custom_call_target="tpu_custom_call" | custom-call | tf_op jit(solution)/shard_map/pallas_call | solution.py:458

commit v2 on v0

--- a/solution.py
+++ b/solution.py
@@ -93,7 +93,8 @@
     return (values, item_grad)
 
 
-CHUNKS = 4
+CHUNKS = 2
+W_COPIES = 8
 
 
 def iota(shape, dim):
@@ -186,14 +187,21 @@
         pl.semaphore_wait(barrier, len(group) + 1)
         pl.semaphore_signal(hello, inc=1, device_id=sibling, device_id_type=MESH)
 
-    w_copy = pltpu.make_async_remote_copy(
-        src_ref=weight, dst_ref=w_buf.at[core], send_sem=w_sem.at[0], recv_sem=w_sem.at[1],
-        device_id=sibling, device_id_type=MESH,
-    )
+    stripe = weight.shape[0] // W_COPIES
+    w_copies = [
+        pltpu.make_async_remote_copy(
+            src_ref=weight.at[pl.ds(k * stripe, stripe)],
+            dst_ref=w_buf.at[core, pl.ds(k * stripe, stripe)],
+            send_sem=w_sem.at[0, k], recv_sem=w_sem.at[1, k],
+            device_id=sibling, device_id_type=MESH,
+        )
+        for k in range(W_COPIES)
+    ]
 
     @pl.when(core == 1)
     def _():
-        w_copy.start()
+        for copy in w_copies:
+            copy.start()
 
     def remote(src, dst, send, recv, target):
         return pltpu.make_async_remote_copy(
@@ -223,8 +231,8 @@
         for k, mate in enumerate(mates):
             remote(into.at[mate], into.at[mate], send.at[k], recv.at[mate], chip_id(mate)).wait_recv()
 
+    send_dp(lambda peer: history_hbm, hist_buf, hist_send, hist_recv)
     loads[0].wait()
-    send_dp(lambda peer: history, hist_buf, hist_send, hist_recv)
     hist_buf[here] = history[...]
 
     loads[1].wait()
@@ -263,6 +271,12 @@
     hidden = hidden_buf[...].astype(f32)
     item_scale = lax.rsqrt(jnp.mean(hidden * hidden, axis=1, keepdims=True) + 1e-6)
     item_emb = (hidden * item_scale * item_gain[...]).astype(bf16)
+
+    @pl.when(core == 0)
+    def _():
+        pl.semaphore_wait(hello, 1)
+        for copy in w_copies:
+            copy.start()
 
     wait_dp(hist_buf, hist_send, hist_recv)
     base = (here * item_rows).astype(f32)
@@ -281,11 +295,6 @@
     send_dp(lambda peer: emb_out.at[peer], emb_in, emb_send, emb_recv)
     emb_in[here] = emb_out[here]
 
-    @pl.when(core == 0)
-    def _():
-        pl.semaphore_wait(hello, 1)
-        w_copy.start()
-
     loads[5].wait()
     wait_dp(emb_in, emb_send, emb_recv)
 
@@ -297,23 +306,38 @@
     send_chip(lambda mate: x_out.at[mate], x_in, x_send, x_recv)
     x_in[chip] = x_out[chip]
 
+    depth = weight.shape[0]
+
+    def half_columns(half):
+        return pl.ds(pl.multiple_of(half * depth, depth), depth)
+
+    def up_half(half):
+        up = jnp.zeros((chips * rows, depth), f32)
+        for c in range(CHUNKS):
+            sums = sum_buf[c].reshape(chips * rows, cols)
+            up = up + dot(sums, w_buf[half, :, c * cols : (c + 1) * cols], 1, 1)
+        up_out[:, :, half_columns(half)] = up.reshape(chips, rows, depth)
+
+    def part_half(half, c):
+        x_half = x_in[:, :, half_columns(half)].reshape(chips * rows, depth)
+        part = dot(x_half, w_buf[half, :, c * cols : (c + 1) * cols])
+        return part.reshape(chips, rows, cols)
+
     loads[6].wait()
-    w_copy.wait()
-    w_all = w_buf[...].reshape(piece, -1)
-
-    up = jnp.zeros((chips * rows, piece), f32)
     for c in range(CHUNKS):
         wait_chip(sum_buf.at[c], sum_send.at[c], sum_recv.at[c])
-        sums = sum_buf[c].reshape(chips * rows, cols)
-        up = up + dot(sums, w_all[:, c * cols : (c + 1) * cols], 1, 1)
-    up_out[...] = up.reshape(chips, rows, piece)
+    up_half(core)
+    wait_chip(x_in, x_send, x_recv)
+    for c in range(CHUNKS):
+        part_own[c] = part_half(core, c)
+
+    for copy in w_copies:
+        copy.wait()
+    up_half(1 - core)
     send_chip(lambda mate: up_out.at[mate], up_in, up_send, up_recv)
     up_in[chip] = up_out[chip]
-
-    wait_chip(x_in, x_send, x_recv)
-    x_all = x_in[...].reshape(chips * rows, piece)
     for c in range(CHUNKS):
-        part = dot(x_all, w_all[:, c * cols : (c + 1) * cols]).reshape(chips, rows, cols)
+        part = part_own[c] + part_half(1 - core, c)
         part_own[c] = part
         part_out[c] = part.astype(bf16)
         send_chip(
@@ -437,7 +461,7 @@
             pltpu.VMEM((CHUNKS, rows, cols), bf16),
             pltpu.VMEM((rows, hist_rows), bf16),
             pltpu.VMEM((item_rows, rows), bf16),
-            dma(7), dma(3 + CHUNKS), dma(2), pltpu.SemaphoreType.REGULAR,
+            dma(7), dma(3 + CHUNKS), dma(2, W_COPIES), pltpu.SemaphoreType.REGULAR,
             dma(groups), dma(groups), dma(groups), dma(groups),
             dma(CHUNKS, chips), dma(CHUNKS, chips), dma(chips), dma(chips),
             dma(CHUNKS, chips), dma(CHUNKS, chips), dma(chips), dma(chips),

time: 30.8 us -> 32.8 us (1.065)
  Pallas kernels: 30 us -> 32 us
    pallas_call x1, Pallas kernels: 27.3 us -> 29.4 us  [local_moving_rows(): pl.pallas_call(functools.partial(kernel, groups, chips), out_shape=(jax.S...]
where the time goes in v2:
time: 32.8 us; the launch traced here: 32.6 us
  Pallas kernels  32 us (98%)
  between operations  0.64 us (2%)
    pallas_call x1, Pallas kernels, local_moving_rows(): pl.pallas_call(functools.partial(kernel, groups, chips), out_shape=(jax.S...  29.4 us
    pallas_call x1, Pallas kernels, local_moving_rows(): pl.pallas_call(functools.partial(finish, groups), out_shape=(jax.ShapeDty...  2.62 us

profile of v2, /device:TPU:0, one launch (start us, length us, event | category | flops | bytes accessed | tf_op | source)
XLA Modules:
  0.0 32.6 jit_solution(2681583374102338677)
XLA Ops:
  0.6 29.4 %shard_map.86 = (bf16[4,16,1024]{2,1,0:T(8,128)(2,1)}, bf16[2,32,1024]{2,1,0:T(8,128)(2,1)}, bf16[32,128]{1,0:T(8,128)(2,1)}, bf16[64,32]{1,0:T(8,128)(2,1)}) custom-call(f32[1,2048]{1,0:T(1,128)} %bitcast.3, s32[1,128]{1,0:T(1,128)} %bitcast.6, s32[1,256]{1,0:T(1,128)} %owner_hbm.1, f32[1,2048]{1,0:T(1,128)} %bitcast.5, bf16[64,2048]{1,0:T(8,128)(2,1)} %hidden_hbm.1, ...), custom_call_target="tpu_custom_call" | custom-call | tf_op jit(solution)/shard_map/pallas_call | solution.py:431
  30.0 2.6 %shard_map.87 = (bf16[128,2048]{1,0:T(8,128)(2,1)}, f32[64,2048]{1,0:T(8,128)}) custom-call(bf16[4,16,1024]{2,1,0:T(8,128)(2,1)} %get-tuple-element.6.back_hbm, bf16[2,32,1024]{2,1,0:T(8,128)(2,1)} %get-tuple-element.7.total_hbm, bf16[32,128]{1,0:T(8,128)(2,1)} %get-tuple-element.8.place_hbm, bf16[64,32]{1,0:T(8,128)(2,1)} %get-tuple-element.9.select_hbm, ...), custom_call_target="tpu_custom_call" | custom-call | tf_op jit(solution)/shard_map/pallas_call | solution.py:477

commit v3 on v0

--- a/solution.py
+++ b/solution.py
@@ -133,12 +133,12 @@
 def kernel(
     groups, chips,
     item_gain_hbm, history_hbm, owner_hbm, user_gain_hbm, item_hidden, weight, value_grad,
-    back_in, total_out, place_out, select_out,
+    back_in, total_in, place_out, select_out,
     item_gain, history, owner, user_gain,
     hidden_buf, grad_buf, w_buf, hist_buf, emb_out, emb_in, sum_buf, x_out, x_in,
     part_own, part_out, part_in, up_out, up_in, back_out, total_buf, place_buf, select_buf,
     local_sem, out_sem, w_sem, hello, hist_send, hist_recv, emb_send, emb_recv, sum_send, sum_recv,
-    x_send, x_recv, part_send, part_recv, up_send, up_recv, back_send, back_recv,
+    x_send, x_recv, part_send, part_recv, up_send, up_recv, back_send, back_recv, total_send, total_recv,
 ):
     here = lax.axis_index("dp")
     fsdp = lax.axis_index("fsdp")
@@ -223,8 +223,8 @@
         for k, mate in enumerate(mates):
             remote(into.at[mate], into.at[mate], send.at[k], recv.at[mate], chip_id(mate)).wait_recv()
 
+    send_dp(lambda peer: history_hbm, hist_buf, hist_send, hist_recv)
     loads[0].wait()
-    send_dp(lambda peer: history, hist_buf, hist_send, hist_recv)
     hist_buf[here] = history[...]
 
     loads[1].wait()
@@ -263,6 +263,10 @@
     hidden = hidden_buf[...].astype(f32)
     item_scale = lax.rsqrt(jnp.mean(hidden * hidden, axis=1, keepdims=True) + 1e-6)
     item_emb = (hidden * item_scale * item_gain[...]).astype(bf16)
+    loads[5].wait()
+    held = item_emb.astype(f32)
+    held_scale = lax.rsqrt(jnp.mean(held * held, axis=1, keepdims=True) + 1e-6)
+    held_normed = (held * held_scale * user_gain[...]).astype(bf16)
 
     wait_dp(hist_buf, hist_send, hist_recv)
     base = (here * item_rows).astype(f32)
@@ -275,6 +279,11 @@
     select_buf[...] = select
     outs.append(pltpu.make_async_copy(select_buf, select_out, out_sem.at[1]))
     outs[1].start()
+    normed = dot(select, held_normed, 0, 0).astype(bf16)
+    for p in range(chips):
+        x_out[p] = normed[:, p * piece : (p + 1) * piece]
+    send_chip(lambda mate: x_out.at[mate], x_in, x_send, x_recv)
+    x_in[chip] = x_out[chip]
     outgoing = dot(select, item_emb, 0, 0)
     for t in range(groups):
         emb_out[t] = fold(outgoing[t * CAP : (t + 1) * CAP]).astype(bf16)
@@ -285,17 +294,6 @@
     def _():
         pl.semaphore_wait(hello, 1)
         w_copy.start()
-
-    loads[5].wait()
-    wait_dp(emb_in, emb_send, emb_recv)
-
-    x = jnp.concatenate([unfold(emb_in[e].astype(f32)) for e in range(groups)], axis=0)
-    scale = lax.rsqrt(jnp.mean(x * x, axis=1, keepdims=True) + 1e-6)
-    normed = (x * scale * user_gain[...]).astype(bf16)
-    for p in range(chips):
-        x_out[p] = normed[:, p * piece : (p + 1) * piece]
-    send_chip(lambda mate: x_out.at[mate], x_in, x_send, x_recv)
-    x_in[chip] = x_out[chip]
 
     loads[6].wait()
     w_copy.wait()
@@ -320,6 +318,9 @@
             lambda mate: part_out.at[c, mate], part_in.at[c], part_send.at[c], part_recv.at[c]
         )
 
+    wait_dp(emb_in, emb_send, emb_recv)
+    x = jnp.concatenate([unfold(emb_in[e].astype(f32)) for e in range(groups)], axis=0)
+    scale = lax.rsqrt(jnp.mean(x * x, axis=1, keepdims=True) + 1e-6)
     wait_chip(up_in, up_send, up_recv)
     upstream = jnp.concatenate([up_in[p] for p in range(chips)], axis=1)
     unit = x * scale
@@ -336,12 +337,20 @@
         total = part_own[c, chip]
         for mate in mates:
             total = total + part_in[c, mate].astype(f32)
-        total_buf[c] = total.astype(bf16)
-        out = pltpu.make_async_copy(total_buf.at[c], total_out.at[c], out_sem.at[3 + c])
+        for t in range(groups):
+            total_buf[c, t] = fold(total[t * CAP : (t + 1) * CAP]).astype(bf16)
+        send_dp(
+            lambda peer: total_buf.at[c, peer], total_in.at[c], total_send.at[c], total_recv.at[c]
+        )
+        out = pltpu.make_async_copy(
+            total_buf.at[c, here], total_in.at[c, here], out_sem.at[3 + c]
+        )
         out.start()
         outs.append(out)
 
     wait_dp(back_in, back_send, back_recv)
+    for c in range(CHUNKS):
+        wait_dp(total_in.at[c], total_send.at[c], total_recv.at[c])
     for out in outs:
         out.wait()
     for copy in sends:
@@ -378,9 +387,11 @@
     loads[4].wait()
     loads[5].wait()
     named = place[...]
-    cols = total.shape[2]
+    cols = values.shape[1] // CHUNKS
     for c in range(CHUNKS):
-        values[:, c * cols : (c + 1) * cols] = dot(named, total[c], 0, 0).astype(bf16)
+        rows = [unfold(total[c, e].astype(f32)) for e in range(groups)]
+        rows = jnp.concatenate(rows, axis=0).astype(bf16)
+        values[:, c * cols : (c + 1) * cols] = dot(named, rows, 0, 0).astype(bf16)
     values_copy = pltpu.make_async_copy(values, values_out, out_sem.at[1])
     values_copy.start()
     grad_copy.wait()
@@ -408,7 +419,7 @@
         functools.partial(kernel, groups, chips),
         out_shape=(
             jax.ShapeDtypeStruct(folded, bf16),
-            jax.ShapeDtypeStruct((CHUNKS, rows, cols), bf16),
+            jax.ShapeDtypeStruct((CHUNKS, groups, 2 * CAP, cols // 2), bf16),
             jax.ShapeDtypeStruct((rows, hist_rows), bf16),
             jax.ShapeDtypeStruct((item_rows, rows), bf16),
         ),
@@ -434,14 +445,14 @@
             pltpu.VMEM((chips, rows, piece), f32),
             pltpu.VMEM((chips, rows, piece), f32),
             pltpu.VMEM(folded, bf16),
-            pltpu.VMEM((CHUNKS, rows, cols), bf16),
+            pltpu.VMEM((CHUNKS, groups, 2 * CAP, cols // 2), bf16),
             pltpu.VMEM((rows, hist_rows), bf16),
             pltpu.VMEM((item_rows, rows), bf16),
             dma(7), dma(3 + CHUNKS), dma(2), pltpu.SemaphoreType.REGULAR,
             dma(groups), dma(groups), dma(groups), dma(groups),
             dma(CHUNKS, chips), dma(CHUNKS, chips), dma(chips), dma(chips),
             dma(CHUNKS, chips), dma(CHUNKS, chips), dma(chips), dma(chips),
-            dma(groups), dma(groups),
+            dma(groups), dma(groups), dma(CHUNKS, groups), dma(CHUNKS, groups),
         ],
         compiler_params=pltpu.CompilerParams(
             collective_id=0, has_side_effects=True, vmem_limit_bytes=60 * 2**20
@@ -460,7 +471,7 @@
         out_specs=(hbm,) * 2,
         scratch_shapes=[
             pltpu.VMEM(folded, bf16),
-            pltpu.VMEM((CHUNKS, rows, cols), bf16),
+            pltpu.VMEM((CHUNKS, groups, 2 * CAP, cols // 2), bf16),
             pltpu.VMEM((rows, hist_rows), bf16),
             pltpu.VMEM((item_rows, rows), bf16),
             pltpu.VMEM((item_rows, width), bf16),

time: 30.8 us -> 34 us (1.10)
  Pallas kernels: 30 us -> 33.2 us
    pallas_call x1, Pallas kernels: 27.3 us -> 30.5 us  [local_moving_rows(): pl.pallas_call(functools.partial(kernel, groups, chips), out_shape=(jax.S...]
where the time goes in v3:
time: 34 us; the launch traced here: 33.8 us
  Pallas kernels  33.2 us (98%)
  between operations  0.64 us (2%)
    pallas_call x1, Pallas kernels, local_moving_rows(): pl.pallas_call(functools.partial(kernel, groups, chips), out_shape=(jax.S...  30.5 us
    pallas_call x1, Pallas kernels, local_moving_rows(): pl.pallas_call(functools.partial(finish, groups), out_shape=(jax.ShapeDty...  2.63 us

profile of v3, /device:TPU:0, one launch (start us, length us, event | category | flops | bytes accessed | tf_op | source)
XLA Modules:
  0.0 33.8 jit_solution(6104464356859656930)
XLA Ops:
  0.6 30.5 %shard_map.86 = (bf16[4,16,1024]{2,1,0:T(8,128)(2,1)}, bf16[4,4,16,256]{3,2,1,0:T(8,128)(2,1)}, bf16[32,128]{1,0:T(8,128)(2,1)}, bf16[64,32]{1,0:T(8,128)(2,1)}) custom-call(f32[1,2048]{1,0:T(1,128)} %bitcast.3, s32[1,128]{1,0:T(1,128)} %bitcast.6, s32[1,256]{1,0:T(1,128)} %owner_hbm.1, f32[1,2048]{1,0:T(1,128)} %bitcast.5, bf16[64,2048]{1,0:T(8,128)(2,1)} %hidden_hbm.1, ...), custom_call_target="tpu_custom_call" | custom-call | tf_op jit(solution)/shard_map/pallas_call | solution.py:418
  31.2 2.6 %shard_map.87 = (bf16[128,2048]{1,0:T(8,128)(2,1)}, f32[64,2048]{1,0:T(8,128)}) custom-call(bf16[4,16,1024]{2,1,0:T(8,128)(2,1)} %get-tuple-element.6.back_hbm, bf16[4,4,16,256]{3,2,1,0:T(8,128)(2,1)} %get-tuple-element.7.total_hbm, bf16[32,128]{1,0:T(8,128)(2,1)} %get-tuple-element.8.place_hbm, bf16[64,32]{1,0:T(8,128)(2,1)} %get-tuple-element.9.select_hbm, ...), custom_call_target="tpu_custom_call" | custom-call | tf_op jit(solution)/shard_map/pallas_call | solution.py:464

commit v4 on v0

--- a/solution.py
+++ b/solution.py
@@ -93,7 +93,7 @@
     return (values, item_grad)
 
 
-CHUNKS = 4
+CHUNKS = 2
 
 
 def iota(shape, dim):
@@ -136,9 +136,9 @@
     back_in, total_out, place_out, select_out,
     item_gain, history, owner, user_gain,
     hidden_buf, grad_buf, w_buf, hist_buf, emb_out, emb_in, sum_buf, x_out, x_in,
-    part_own, part_out, part_in, up_out, up_in, back_out, total_buf, place_buf, select_buf,
+    part_own, part_out, part_in, back_out, total_buf, place_buf, select_buf,
     local_sem, out_sem, w_sem, hello, hist_send, hist_recv, emb_send, emb_recv, sum_send, sum_recv,
-    x_send, x_recv, part_send, part_recv, up_send, up_recv, back_send, back_recv,
+    x_send, x_recv, part_send, part_recv, back_send, back_recv,
 ):
     here = lax.axis_index("dp")
     fsdp = lax.axis_index("fsdp")
@@ -161,7 +161,11 @@
     sibling = (here, chip * 2 + 1 - core)
 
     barrier = pltpu.get_barrier_semaphore()
-    group = [dp_id(p) for p in peers] + [chip_id(m) for m in mates]
+    others = [
+        (lax.rem(here + i, groups), lax.rem(chip + j, chips))
+        for i in range(groups) for j in range(chips) if i or j
+    ]
+    group = [(peer, mate * 2 + core) for peer, mate in others]
     for target in group:
         pl.semaphore_signal(barrier, inc=1, device_id=target, device_id_type=MESH)
 
@@ -223,8 +227,8 @@
         for k, mate in enumerate(mates):
             remote(into.at[mate], into.at[mate], send.at[k], recv.at[mate], chip_id(mate)).wait_recv()
 
+    send_dp(lambda peer: history_hbm, hist_buf, hist_send, hist_recv)
     loads[0].wait()
-    send_dp(lambda peer: history, hist_buf, hist_send, hist_recv)
     hist_buf[here] = history[...]
 
     loads[1].wait()
@@ -306,9 +310,21 @@
         wait_chip(sum_buf.at[c], sum_send.at[c], sum_recv.at[c])
         sums = sum_buf[c].reshape(chips * rows, cols)
         up = up + dot(sums, w_all[:, c * cols : (c + 1) * cols], 1, 1)
-    up_out[...] = up.reshape(chips, rows, piece)
-    send_chip(lambda mate: up_out.at[mate], up_in, up_send, up_recv)
-    up_in[chip] = up_out[chip]
+    for m in range(chips):
+        for e in range(groups):
+            at = m * rows + e * CAP
+            back_out[e, m] = fold(up[at : at + CAP]).astype(bf16)
+    for peer, mate in others:
+        copy = remote(
+            back_out.at[peer, mate], back_in.at[here, chip],
+            back_send.at[peer, mate], back_recv.at[here, chip], (peer, mate * 2 + core),
+        )
+        copy.start()
+        sends.append(copy)
+    outs.append(pltpu.make_async_copy(
+        back_out.at[here, chip], back_in.at[here, chip], out_sem.at[2]
+    ))
+    outs[2].start()
 
     wait_chip(x_in, x_send, x_recv)
     x_all = x_in[...].reshape(chips * rows, piece)
@@ -320,17 +336,6 @@
             lambda mate: part_out.at[c, mate], part_in.at[c], part_send.at[c], part_recv.at[c]
         )
 
-    wait_chip(up_in, up_send, up_recv)
-    upstream = jnp.concatenate([up_in[p] for p in range(chips)], axis=1)
-    unit = x * scale
-    scaled = upstream * user_gain[...]
-    block_sum = scale * (scaled - unit * jnp.mean(scaled * unit, axis=1, keepdims=True))
-    for t in range(groups):
-        back_out[t] = fold(block_sum[t * CAP : (t + 1) * CAP]).astype(bf16)
-    send_dp(lambda peer: back_out.at[peer], back_in, back_send, back_recv)
-    outs.append(pltpu.make_async_copy(back_out.at[here], back_in.at[here], out_sem.at[2]))
-    outs[2].start()
-
     for c in range(CHUNKS):
         wait_chip(part_in.at[c], part_send.at[c], part_recv.at[c])
         total = part_own[c, chip]
@@ -341,7 +346,11 @@
         out.start()
         outs.append(out)
 
-    wait_dp(back_in, back_send, back_recv)
+    for peer, mate in others:
+        remote(
+            back_in.at[peer, mate], back_in.at[peer, mate],
+            back_send.at[peer, mate], back_recv.at[peer, mate], (peer, mate * 2 + core),
+        ).wait_recv()
     for out in outs:
         out.wait()
     for copy in sends:
@@ -349,15 +358,16 @@
 
 
 def finish(
-    groups, back_hbm, total_hbm, place_hbm, select_hbm, hidden_hbm, gain_hbm,
+    groups, chips,
+    back_hbm, total_hbm, place_hbm, select_hbm, hidden_hbm, gain_hbm, user_gain_hbm,
     values_out, item_grad_out,
-    back, total, place, select, hidden_buf, gain, values, item_grad, load_sem, out_sem,
+    back, total, place, select, hidden_buf, gain, user_gain, values, item_grad, load_sem, out_sem,
 ):
     loads = [
         pltpu.make_async_copy(src, dst, load_sem.at[k])
         for k, (src, dst) in enumerate([
             (hidden_hbm, hidden_buf), (gain_hbm, gain), (select_hbm, select), (back_hbm, back),
-            (place_hbm, place), (total_hbm, total),
+            (place_hbm, place), (total_hbm, total), (user_gain_hbm, user_gain),
         ])
     ]
     for load in loads:
@@ -366,11 +376,20 @@
     loads[1].wait()
     hidden = hidden_buf[...].astype(f32)
     scale = lax.rsqrt(jnp.mean(hidden * hidden, axis=1, keepdims=True) + 1e-6)
-    loads[2].wait()
-    loads[3].wait()
-    returned = jnp.concatenate([unfold(back[t].astype(f32)) for t in range(groups)], axis=0)
-    emb_grad = dot(select[...], returned.astype(bf16))
     unit = hidden * scale
+    emb = (unit * gain[...]).astype(bf16).astype(f32)
+    emb_scale = lax.rsqrt(jnp.mean(emb * emb, axis=1, keepdims=True) + 1e-6)
+    emb_unit = emb * emb_scale
+    for load in (loads[2], loads[3], loads[6]):
+        load.wait()
+    returned = jnp.concatenate([
+        jnp.concatenate([unfold(back[t, q].astype(f32)) for q in range(chips)], axis=1)
+        for t in range(groups)
+    ], axis=0)
+    scaled = dot(select[...], returned.astype(bf16)) * user_gain[...]
+    emb_grad = emb_scale * (
+        scaled - emb_unit * jnp.mean(scaled * emb_unit, axis=1, keepdims=True)
+    )
     scaled = emb_grad * gain[...]
     item_grad[...] = scale * (scaled - unit * jnp.mean(scaled * unit, axis=1, keepdims=True))
     grad_copy = pltpu.make_async_copy(item_grad, item_grad_out, out_sem.at[0])
@@ -404,10 +423,11 @@
         return pltpu.SemaphoreType.DMA(counts)
 
     folded = (groups, 2 * CAP, width // 2)
+    slices = (groups, chips, 2 * CAP, piece // 2)
     back, total, place, select = pl.pallas_call(
         functools.partial(kernel, groups, chips),
         out_shape=(
-            jax.ShapeDtypeStruct(folded, bf16),
+            jax.ShapeDtypeStruct(slices, bf16),
             jax.ShapeDtypeStruct((CHUNKS, rows, cols), bf16),
             jax.ShapeDtypeStruct((rows, hist_rows), bf16),
             jax.ShapeDtypeStruct((item_rows, rows), bf16),
@@ -431,17 +451,14 @@
             pltpu.VMEM((CHUNKS, chips, rows, cols), f32),
             pltpu.VMEM((CHUNKS, chips, rows, cols), bf16),
             pltpu.VMEM((CHUNKS, chips, rows, cols), bf16),
-            pltpu.VMEM((chips, rows, piece), f32),
-            pltpu.VMEM((chips, rows, piece), f32),
-            pltpu.VMEM(folded, bf16),
+            pltpu.VMEM(slices, bf16),
             pltpu.VMEM((CHUNKS, rows, cols), bf16),
             pltpu.VMEM((rows, hist_rows), bf16),
             pltpu.VMEM((item_rows, rows), bf16),
             dma(7), dma(3 + CHUNKS), dma(2), pltpu.SemaphoreType.REGULAR,
             dma(groups), dma(groups), dma(groups), dma(groups),
             dma(CHUNKS, chips), dma(CHUNKS, chips), dma(chips), dma(chips),
-            dma(CHUNKS, chips), dma(CHUNKS, chips), dma(chips), dma(chips),
-            dma(groups), dma(groups),
+            dma(CHUNKS, chips), dma(CHUNKS, chips), dma(groups, chips), dma(groups, chips),
         ],
         compiler_params=pltpu.CompilerParams(
             collective_id=0, has_side_effects=True, vmem_limit_bytes=60 * 2**20
@@ -451,26 +468,27 @@
         item_hidden, value_weight, value_grad,
     )
     return pl.pallas_call(
-        functools.partial(finish, groups),
+        functools.partial(finish, groups, chips),
         out_shape=(
             jax.ShapeDtypeStruct((hist_rows, out_width), bf16),
             jax.ShapeDtypeStruct((item_rows, width), f32),
         ),
-        in_specs=[hbm] * 6,
+        in_specs=[hbm] * 7,
         out_specs=(hbm,) * 2,
         scratch_shapes=[
-            pltpu.VMEM(folded, bf16),
+            pltpu.VMEM(slices, bf16),
             pltpu.VMEM((CHUNKS, rows, cols), bf16),
             pltpu.VMEM((rows, hist_rows), bf16),
             pltpu.VMEM((item_rows, rows), bf16),
             pltpu.VMEM((item_rows, width), bf16),
             pltpu.VMEM((1, width), f32),
+            pltpu.VMEM((1, width), f32),
             pltpu.VMEM((hist_rows, out_width), bf16),
             pltpu.VMEM((item_rows, width), f32),
-            dma(6), dma(2),
+            dma(7), dma(2),
         ],
         compiler_params=pltpu.CompilerParams(vmem_limit_bytes=60 * 2**20),
-    )(back, total, place, select, item_hidden, item_gain[None, :])
+    )(back, total, place, select, item_hidden, item_gain[None, :], user_gain[None, :])
 
 
 def local(item_hidden, item_gain, history, owner_map, user_gain, value_weight, value_grad):

time: 30.8 us -> 31.5 us (1.023)
  Pallas kernels: 30 us -> 30.7 us
    pallas_call x1, Pallas kernels: 27.3 us -> 27.8 us  [local_moving_rows(): pl.pallas_call(functools.partial(kernel, groups, chips), out_shape=(jax.S...]
where the time goes in v4:
time: 31.5 us; the launch traced here: 31.4 us
  Pallas kernels  30.7 us (97%)
  between operations  0.64 us (2%)
    pallas_call x1, Pallas kernels, local_moving_rows(): pl.pallas_call(functools.partial(kernel, groups, chips), out_shape=(jax.S...  27.8 us
    pallas_call x1, Pallas kernels, local_moving_rows(): pl.pallas_call(functools.partial(finish, groups, chips), out_shape=(jax.S...  2.93 us

profile of v4, /device:TPU:0, one launch (start us, length us, event | category | flops | bytes accessed | tf_op | source)
XLA Modules:
  0.0 31.4 jit_solution(17427415368899220385)
XLA Ops:
  0.6 27.8 %shard_map.86 = (bf16[4,4,16,256]{3,2,1,0:T(8,128)(2,1)}, bf16[2,32,1024]{2,1,0:T(8,128)(2,1)}, bf16[32,128]{1,0:T(8,128)(2,1)}, bf16[64,32]{1,0:T(8,128)(2,1)}) custom-call(f32[1,2048]{1,0:T(1,128)} %bitcast.3, s32[1,128]{1,0:T(1,128)} %bitcast.7, s32[1,256]{1,0:T(1,128)} %owner_hbm.1, f32[1,2048]{1,0:T(1,128)} %bitcast.5, bf16[64,2048]{1,0:T(8,128)(2,1)} %hidden_hbm.1, ...), custom_call_target="tpu_custom_call" | custom-call | tf_op jit(solution)/shard_map/pallas_call | solution.py:427
  28.4 2.9 %shard_map.87 = (bf16[128,2048]{1,0:T(8,128)(2,1)}, f32[64,2048]{1,0:T(8,128)}) custom-call(bf16[4,4,16,256]{3,2,1,0:T(8,128)(2,1)} %get-tuple-element.6.back_hbm, bf16[2,32,1024]{2,1,0:T(8,128)(2,1)} %get-tuple-element.7.total_hbm, bf16[32,128]{1,0:T(8,128)(2,1)} %get-tuple-element.8.place_hbm, bf16[64,32]{1,0:T(8,128)(2,1)} %get-tuple-element.9.select_hbm, ...), custom_call_target="tpu_custom_call" | custom-call | tf_op jit(solution)/shard_map/pallas_call | solution.py:470
